TPU v7x, 512 devices: a whole 4x4x16 slice. The times are simulated.
512 devices in a mesh: row: 8 (over y, z_hi), col: 16 (over z_lo, core), rep: 4 (over x).
Axes of the slice: x: 4, y: 4, z: 16 (z_hi: 2, z_lo: 8; z = z_hi * 8 + z_lo), core: 2. Of those that a mesh axis runs over, the one named last changes fastest.
Arguments:
- amplitudes: float32 [18432, 18432], P('row', ('col', 'rep')), may hold values from -0.046875 to 0.046875
- cycle_ints: float32 [18432, 1152], P(('col', 'rep'), 'row'), may hold values from -16 to 16
Outputs:
- cycle_term: float32 [18432, 1152], P(('row', 'rep'), 'col')
All inputs are finite; a program needn't handle non-finite values.
Results may differ from a plain program's by a relative error of at most 0.0002.
Values sent between devices are 32-bit elements; how exact they have to be, the bound alone decides.
A program may use at most 64 MiB of HBM per device.

v0:
```python
import jax
import jax.numpy as jnp
from jax import lax
from jax.sharding import PartitionSpec as P


def passed_along(x, axis, by):
    devices = lax.axis_size(axis)
    return lax.ppermute(x, axis, [(i, (i + by) % devices) for i in range(devices)])


def per_device(amplitudes, cycle_ints):
    n_col = lax.axis_size("col")
    full_ints = lax.all_gather(cycle_ints, "row", axis=1, tiled=True)
    width = full_ints.shape[1] // n_col
    here = lax.axis_index("col")
    n_rows = amplitudes.shape[0]

    def product(block, offset, count):
        columns = lax.dynamic_slice_in_dim(full_ints, block * width + offset, count, 1)
        return jnp.dot(
            amplitudes, columns, precision=lax.Precision.HIGHEST, preferred_element_type=jnp.float32
        )

    def advance(step, partial_sum):
        block = (here - step) % n_col
        partial_sum = partial_sum + product(block, 0, width)
        return passed_along(partial_sum, "col", 1)

    totals = lax.fori_loop(0, n_col, advance, jnp.zeros((n_rows, width), jnp.float32))
    return lax.psum_scatter(totals, "rep", scatter_dimension=0, tiled=True)


def solution(mesh):
    return jax.shard_map(
        per_device,
        mesh=mesh,
        in_specs=(P("row", ("col", "rep")), P(("col", "rep"), "row")),
        out_specs=P(("row", "rep"), "col"),
        check_vma=False,
    )
```

profile of v0, /device:TPU:16, one launch (start us, length us, event | category | flops | bytes accessed | tf_op | source)
XLA Modules:
  0.0 518.8 jit_solution(9716333784777481202)
XLA Ops:
  6.5 0.0 all-gather.2.cloned.1.call-start
  6.5 0.7 all-gather.2.cloned.1.call-update
  7.3 0.0 reduce-scatter.4.cloned.1.call-start
  7.3 116.6 %all-gather.2.cloned.1.call-done = f32[288,1152]{0,1:T(8,128)} async-done(((f32[288,144]{0,1:T(8,128)}), f32[288,1152]{0,1:T(8,128)}) %all-gather.2.cloned.1.call-update) | async-done | bytes 1327120 | tf_op jit(solution)/shard_map/all_gather | solution.py:14
  123.9 360.8 %while.15 = (s32[]{:T(128)}, f32[2304,72]{0,1:T(8,128)S(1)}, s32[]{:T(128)}, f32[288,1152]{0,1:T(8,128)}, f32[2304,288]{0,1:T(8,128)}, /*index=5*/s32[]{:T(128)}...) while((s32[]{:T(128)}, f32[2304,72]{0,1:T(8,128)S(1)}, s32[]{:T(128)}, ...), condition=%wide.region_1.2_spmd, body=%wide.region_0.1_spmd.sunk | while | flops 573474816 | bytes 6746432 | solution.py:30
  124.0 3.9 fusion.9
  127.9 1.9 collective-permute-start
  129.8 16.7 %collective-permute-done = f32[2304,72]{0,1:T(8,128)S(1)} collective-permute-done((f32[2304,72]{0,1:T(8,128)S(1)}, f32[2304,72]{0,1:T(8,128)S(1)}, u32[]{:S(2)}, u32[]{:S(2)}) %collective-permute-start) | collective-permute-done | bytes 663584 | tf_op jit(solution)/shard_map/while/body/eval_jaxpr/ppermute | solution.py:9
  146.5 3.9 fusion.9
  150.5 1.9 collective-permute-start
  152.4 16.7 %collective-permute-done = f32[2304,72]{0,1:T(8,128)S(1)} collective-permute-done((f32[2304,72]{0,1:T(8,128)S(1)}, f32[2304,72]{0,1:T(8,128)S(1)}, u32[]{:S(2)}, u32[]{:S(2)}) %collective-permute-start) | collective-permute-done | bytes 663584 | tf_op jit(solution)/shard_map/while/body/eval_jaxpr/ppermute | solution.py:9
  169.1 3.9 fusion.9
  173.0 1.9 collective-permute-start
  174.9 16.7 %collective-permute-done = f32[2304,72]{0,1:T(8,128)S(1)} collective-permute-done((f32[2304,72]{0,1:T(8,128)S(1)}, f32[2304,72]{0,1:T(8,128)S(1)}, u32[]{:S(2)}, u32[]{:S(2)}) %collective-permute-start) | collective-permute-done | bytes 663584 | tf_op jit(solution)/shard_map/while/body/eval_jaxpr/ppermute | solution.py:9
  191.6 3.9 fusion.9
  195.5 1.9 collective-permute-start
  197.5 16.7 %collective-permute-done = f32[2304,72]{0,1:T(8,128)S(1)} collective-permute-done((f32[2304,72]{0,1:T(8,128)S(1)}, f32[2304,72]{0,1:T(8,128)S(1)}, u32[]{:S(2)}, u32[]{:S(2)}) %collective-permute-start) | collective-permute-done | bytes 663584 | tf_op jit(solution)/shard_map/while/body/eval_jaxpr/ppermute | solution.py:9
  214.1 3.9 fusion.9
  218.1 1.9 collective-permute-start
  220.0 16.7 %collective-permute-done = f32[2304,72]{0,1:T(8,128)S(1)} collective-permute-done((f32[2304,72]{0,1:T(8,128)S(1)}, f32[2304,72]{0,1:T(8,128)S(1)}, u32[]{:S(2)}, u32[]{:S(2)}) %collective-permute-start) | collective-permute-done | bytes 663584 | tf_op jit(solution)/shard_map/while/body/eval_jaxpr/ppermute | solution.py:9
  236.7 3.9 fusion.9
  240.6 1.9 collective-permute-start
  242.6 16.7 %collective-permute-done = f32[2304,72]{0,1:T(8,128)S(1)} collective-permute-done((f32[2304,72]{0,1:T(8,128)S(1)}, f32[2304,72]{0,1:T(8,128)S(1)}, u32[]{:S(2)}, u32[]{:S(2)}) %collective-permute-start) | collective-permute-done | bytes 663584 | tf_op jit(solution)/shard_map/while/body/eval_jaxpr/ppermute | solution.py:9
  259.2 3.9 fusion.9
  263.2 1.9 collective-permute-start
  265.1 16.7 %collective-permute-done = f32[2304,72]{0,1:T(8,128)S(1)} collective-permute-done((f32[2304,72]{0,1:T(8,128)S(1)}, f32[2304,72]{0,1:T(8,128)S(1)}, u32[]{:S(2)}, u32[]{:S(2)}) %collective-permute-start) | collective-permute-done | bytes 663584 | tf_op jit(solution)/shard_map/while/body/eval_jaxpr/ppermute | solution.py:9
  281.8 3.9 fusion.9
  285.7 1.9 collective-permute-start
  287.7 16.7 %collective-permute-done = f32[2304,72]{0,1:T(8,128)S(1)} collective-permute-done((f32[2304,72]{0,1:T(8,128)S(1)}, f32[2304,72]{0,1:T(8,128)S(1)}, u32[]{:S(2)}, u32[]{:S(2)}) %collective-permute-start) | collective-permute-done | bytes 663584 | tf_op jit(solution)/shard_map/while/body/eval_jaxpr/ppermute | solution.py:9
  304.3 3.9 fusion.9
  308.3 1.9 collective-permute-start
  310.2 16.7 %collective-permute-done = f32[2304,72]{0,1:T(8,128)S(1)} collective-permute-done((f32[2304,72]{0,1:T(8,128)S(1)}, f32[2304,72]{0,1:T(8,128)S(1)}, u32[]{:S(2)}, u32[]{:S(2)}) %collective-permute-start) | collective-permute-done | bytes 663584 | tf_op jit(solution)/shard_map/while/body/eval_jaxpr/ppermute | solution.py:9
  326.9 3.9 fusion.9
  330.8 1.9 collective-permute-start
  332.8 16.7 %collective-permute-done = f32[2304,72]{0,1:T(8,128)S(1)} collective-permute-done((f32[2304,72]{0,1:T(8,128)S(1)}, f32[2304,72]{0,1:T(8,128)S(1)}, u32[]{:S(2)}, u32[]{:S(2)}) %collective-permute-start) | collective-permute-done | bytes 663584 | tf_op jit(solution)/shard_map/while/body/eval_jaxpr/ppermute | solution.py:9
  349.4 3.9 fusion.9
  353.4 1.9 collective-permute-start
  355.3 16.7 %collective-permute-done = f32[2304,72]{0,1:T(8,128)S(1)} collective-permute-done((f32[2304,72]{0,1:T(8,128)S(1)}, f32[2304,72]{0,1:T(8,128)S(1)}, u32[]{:S(2)}, u32[]{:S(2)}) %collective-permute-start) | collective-permute-done | bytes 663584 | tf_op jit(solution)/shard_map/while/body/eval_jaxpr/ppermute | solution.py:9
  372.0 3.9 fusion.9
  375.9 1.9 collective-permute-start
  377.8 16.7 %collective-permute-done = f32[2304,72]{0,1:T(8,128)S(1)} collective-permute-done((f32[2304,72]{0,1:T(8,128)S(1)}, f32[2304,72]{0,1:T(8,128)S(1)}, u32[]{:S(2)}, u32[]{:S(2)}) %collective-permute-start) | collective-permute-done | bytes 663584 | tf_op jit(solution)/shard_map/while/body/eval_jaxpr/ppermute | solution.py:9
  394.5 3.9 fusion.9
  398.5 1.9 collective-permute-start
  400.4 16.7 %collective-permute-done = f32[2304,72]{0,1:T(8,128)S(1)} collective-permute-done((f32[2304,72]{0,1:T(8,128)S(1)}, f32[2304,72]{0,1:T(8,128)S(1)}, u32[]{:S(2)}, u32[]{:S(2)}) %collective-permute-start) | collective-permute-done | bytes 663584 | tf_op jit(solution)/shard_map/while/body/eval_jaxpr/ppermute | solution.py:9
  417.1 3.9 fusion.9
  421.0 1.9 collective-permute-start
  422.9 16.7 %collective-permute-done = f32[2304,72]{0,1:T(8,128)S(1)} collective-permute-done((f32[2304,72]{0,1:T(8,128)S(1)}, f32[2304,72]{0,1:T(8,128)S(1)}, u32[]{:S(2)}, u32[]{:S(2)}) %collective-permute-start) | collective-permute-done | bytes 663584 | tf_op jit(solution)/shard_map/while/body/eval_jaxpr/ppermute | solution.py:9
  439.6 3.9 fusion.9
  443.6 1.9 collective-permute-start
  445.5 16.7 %collective-permute-done = f32[2304,72]{0,1:T(8,128)S(1)} collective-permute-done((f32[2304,72]{0,1:T(8,128)S(1)}, f32[2304,72]{0,1:T(8,128)S(1)}, u32[]{:S(2)}, u32[]{:S(2)}) %collective-permute-start) | collective-permute-done | bytes 663584 | tf_op jit(solution)/shard_map/while/body/eval_jaxpr/ppermute | solution.py:9
  462.1 3.9 fusion.9
  466.1 1.9 collective-permute-start
  468.0 16.7 %collective-permute-done = f32[2304,72]{0,1:T(8,128)S(1)} collective-permute-done((f32[2304,72]{0,1:T(8,128)S(1)}, f32[2304,72]{0,1:T(8,128)S(1)}, u32[]{:S(2)}, u32[]{:S(2)}) %collective-permute-start) | collective-permute-done | bytes 663584 | tf_op jit(solution)/shard_map/while/body/eval_jaxpr/ppermute | solution.py:9
  484.7 1.4 copy.5
  486.1 0.0 reduce-scatter.4.cloned.1.call-update
  486.1 24.0 %reduce-scatter.4.cloned.1.call-done = f32[576,72]{1,0:T(8,128)} async-done(((f32[2304,72]{1,0:T(8,128)}), f32[576,72]{1,0:T(8,128)}) %reduce-scatter.4.cloned.1.call-update) | async-done | bytes 165904
  510.1 1.8 copy.6
  (1 shorter events, 0.0 us)
Async XLA Ops:
  6.5 117.3 %all-gather.2.cloned.1.call-start = ((), (), s32[]{:S(2)}) async-start(), calls=%async_computation.1 | async-start | bytes 1990656 | tf_op jit(solution)/shard_map/all_gather | solution.py:14
  7.3 502.9 %reduce-scatter.4.cloned.1.call-start = ((), (), s32[]{:S(2)}) async-start(), calls=%async_computation.2 | async-start | bytes 1474560
  127.9 18.6 %collective-permute-start = (f32[2304,72]{0,1:T(8,128)S(1)}, f32[2304,72]{0,1:T(8,128)S(1)}, u32[]{:S(2)}, u32[]{:S(2)}) collective-permute-start(f32[2304,72]{0,1:T(8,128)S(1)} %fusion.9), channel_id=1, source_target_pairs={{0,4},{4,8},{8,12},{12,16},{16,20},{20,24},{24,28},{28,32},{32,36}... | collective-permute-start | bytes 1990664 | tf_op jit(solution)/shard_map/while/body/eval_jaxpr/ppermute | solution.py:9
  150.5 18.6 %collective-permute-start = (f32[2304,72]{0,1:T(8,128)S(1)}, f32[2304,72]{0,1:T(8,128)S(1)}, u32[]{:S(2)}, u32[]{:S(2)}) collective-permute-start(f32[2304,72]{0,1:T(8,128)S(1)} %fusion.9), channel_id=1, source_target_pairs={{0,4},{4,8},{8,12},{12,16},{16,20},{20,24},{24,28},{28,32},{32,36}... | collective-permute-start | bytes 1990664 | tf_op jit(solution)/shard_map/while/body/eval_jaxpr/ppermute | solution.py:9
  173.0 18.6 %collective-permute-start = (f32[2304,72]{0,1:T(8,128)S(1)}, f32[2304,72]{0,1:T(8,128)S(1)}, u32[]{:S(2)}, u32[]{:S(2)}) collective-permute-start(f32[2304,72]{0,1:T(8,128)S(1)} %fusion.9), channel_id=1, source_target_pairs={{0,4},{4,8},{8,12},{12,16},{16,20},{20,24},{24,28},{28,32},{32,36}... | collective-permute-start | bytes 1990664 | tf_op jit(solution)/shard_map/while/body/eval_jaxpr/ppermute | solution.py:9
  195.5 18.6 %collective-permute-start = (f32[2304,72]{0,1:T(8,128)S(1)}, f32[2304,72]{0,1:T(8,128)S(1)}, u32[]{:S(2)}, u32[]{:S(2)}) collective-permute-start(f32[2304,72]{0,1:T(8,128)S(1)} %fusion.9), channel_id=1, source_target_pairs={{0,4},{4,8},{8,12},{12,16},{16,20},{20,24},{24,28},{28,32},{32,36}... | collective-permute-start | bytes 1990664 | tf_op jit(solution)/shard_map/while/body/eval_jaxpr/ppermute | solution.py:9
  218.1 18.6 %collective-permute-start = (f32[2304,72]{0,1:T(8,128)S(1)}, f32[2304,72]{0,1:T(8,128)S(1)}, u32[]{:S(2)}, u32[]{:S(2)}) collective-permute-start(f32[2304,72]{0,1:T(8,128)S(1)} %fusion.9), channel_id=1, source_target_pairs={{0,4},{4,8},{8,12},{12,16},{16,20},{20,24},{24,28},{28,32},{32,36}... | collective-permute-start | bytes 1990664 | tf_op jit(solution)/shard_map/while/body/eval_jaxpr/ppermute | solution.py:9
  240.6 18.6 %collective-permute-start = (f32[2304,72]{0,1:T(8,128)S(1)}, f32[2304,72]{0,1:T(8,128)S(1)}, u32[]{:S(2)}, u32[]{:S(2)}) collective-permute-start(f32[2304,72]{0,1:T(8,128)S(1)} %fusion.9), channel_id=1, source_target_pairs={{0,4},{4,8},{8,12},{12,16},{16,20},{20,24},{24,28},{28,32},{32,36}... | collective-permute-start | bytes 1990664 | tf_op jit(solution)/shard_map/while/body/eval_jaxpr/ppermute | solution.py:9
  263.2 18.6 %collective-permute-start = (f32[2304,72]{0,1:T(8,128)S(1)}, f32[2304,72]{0,1:T(8,128)S(1)}, u32[]{:S(2)}, u32[]{:S(2)}) collective-permute-start(f32[2304,72]{0,1:T(8,128)S(1)} %fusion.9), channel_id=1, source_target_pairs={{0,4},{4,8},{8,12},{12,16},{16,20},{20,24},{24,28},{28,32},{32,36}... | collective-permute-start | bytes 1990664 | tf_op jit(solution)/shard_map/while/body/eval_jaxpr/ppermute | solution.py:9
  285.7 18.6 %collective-permute-start = (f32[2304,72]{0,1:T(8,128)S(1)}, f32[2304,72]{0,1:T(8,128)S(1)}, u32[]{:S(2)}, u32[]{:S(2)}) collective-permute-start(f32[2304,72]{0,1:T(8,128)S(1)} %fusion.9), channel_id=1, source_target_pairs={{0,4},{4,8},{8,12},{12,16},{16,20},{20,24},{24,28},{28,32},{32,36}... | collective-permute-start | bytes 1990664 | tf_op jit(solution)/shard_map/while/body/eval_jaxpr/ppermute | solution.py:9
  308.3 18.6 %collective-permute-start = (f32[2304,72]{0,1:T(8,128)S(1)}, f32[2304,72]{0,1:T(8,128)S(1)}, u32[]{:S(2)}, u32[]{:S(2)}) collective-permute-start(f32[2304,72]{0,1:T(8,128)S(1)} %fusion.9), channel_id=1, source_target_pairs={{0,4},{4,8},{8,12},{12,16},{16,20},{20,24},{24,28},{28,32},{32,36}... | collective-permute-start | bytes 1990664 | tf_op jit(solution)/shard_map/while/body/eval_jaxpr/ppermute | solution.py:9
  330.8 18.6 %collective-permute-start = (f32[2304,72]{0,1:T(8,128)S(1)}, f32[2304,72]{0,1:T(8,128)S(1)}, u32[]{:S(2)}, u32[]{:S(2)}) collective-permute-start(f32[2304,72]{0,1:T(8,128)S(1)} %fusion.9), channel_id=1, source_target_pairs={{0,4},{4,8},{8,12},{12,16},{16,20},{20,24},{24,28},{28,32},{32,36}... | collective-permute-start | bytes 1990664 | tf_op jit(solution)/shard_map/while/body/eval_jaxpr/ppermute | solution.py:9
  353.4 18.6 %collective-permute-start = (f32[2304,72]{0,1:T(8,128)S(1)}, f32[2304,72]{0,1:T(8,128)S(1)}, u32[]{:S(2)}, u32[]{:S(2)}) collective-permute-start(f32[2304,72]{0,1:T(8,128)S(1)} %fusion.9), channel_id=1, source_target_pairs={{0,4},{4,8},{8,12},{12,16},{16,20},{20,24},{24,28},{28,32},{32,36}... | collective-permute-start | bytes 1990664 | tf_op jit(solution)/shard_map/while/body/eval_jaxpr/ppermute | solution.py:9
  375.9 18.6 %collective-permute-start = (f32[2304,72]{0,1:T(8,128)S(1)}, f32[2304,72]{0,1:T(8,128)S(1)}, u32[]{:S(2)}, u32[]{:S(2)}) collective-permute-start(f32[2304,72]{0,1:T(8,128)S(1)} %fusion.9), channel_id=1, source_target_pairs={{0,4},{4,8},{8,12},{12,16},{16,20},{20,24},{24,28},{28,32},{32,36}... | collective-permute-start | bytes 1990664 | tf_op jit(solution)/shard_map/while/body/eval_jaxpr/ppermute | solution.py:9
  398.5 18.6 %collective-permute-start = (f32[2304,72]{0,1:T(8,128)S(1)}, f32[2304,72]{0,1:T(8,128)S(1)}, u32[]{:S(2)}, u32[]{:S(2)}) collective-permute-start(f32[2304,72]{0,1:T(8,128)S(1)} %fusion.9), channel_id=1, source_target_pairs={{0,4},{4,8},{8,12},{12,16},{16,20},{20,24},{24,28},{28,32},{32,36}... | collective-permute-start | bytes 1990664 | tf_op jit(solution)/shard_map/while/body/eval_jaxpr/ppermute | solution.py:9
  421.0 18.6 %collective-permute-start = (f32[2304,72]{0,1:T(8,128)S(1)}, f32[2304,72]{0,1:T(8,128)S(1)}, u32[]{:S(2)}, u32[]{:S(2)}) collective-permute-start(f32[2304,72]{0,1:T(8,128)S(1)} %fusion.9), channel_id=1, source_target_pairs={{0,4},{4,8},{8,12},{12,16},{16,20},{20,24},{24,28},{28,32},{32,36}... | collective-permute-start | bytes 1990664 | tf_op jit(solution)/shard_map/while/body/eval_jaxpr/ppermute | solution.py:9
  443.6 18.6 %collective-permute-start = (f32[2304,72]{0,1:T(8,128)S(1)}, f32[2304,72]{0,1:T(8,128)S(1)}, u32[]{:S(2)}, u32[]{:S(2)}) collective-permute-start(f32[2304,72]{0,1:T(8,128)S(1)} %fusion.9), channel_id=1, source_target_pairs={{0,4},{4,8},{8,12},{12,16},{16,20},{20,24},{24,28},{28,32},{32,36}... | collective-permute-start | bytes 1990664 | tf_op jit(solution)/shard_map/while/body/eval_jaxpr/ppermute | solution.py:9
  466.1 18.6 %collective-permute-start = (f32[2304,72]{0,1:T(8,128)S(1)}, f32[2304,72]{0,1:T(8,128)S(1)}, u32[]{:S(2)}, u32[]{:S(2)}) collective-permute-start(f32[2304,72]{0,1:T(8,128)S(1)} %fusion.9), channel_id=1, source_target_pairs={{0,4},{4,8},{8,12},{12,16},{16,20},{20,24},{24,28},{28,32},{32,36}... | collective-permute-start | bytes 1990664 | tf_op jit(solution)/shard_map/while/body/eval_jaxpr/ppermute | solution.py:9
Sparse Core Ops, SparseCore 0:
  10.5 113.2 all-gather.1
  486.2 23.8 reduce-scatter.3
where the time goes:
time: 520 us; the launch traced here: 519 us
  waiting for transfers between devices  408 us (78%)
  matrix products  63.1 us (12%)
  starting transfers between devices  30.8 us (6%)
  between operations  13.4 us (3%)
    ppermute x16, waiting for transfers between devices, passed_along(): lax.ppermute(x, axis, [(i, (i + by) % devices) for i in range(devices)])  267 us
    all_gather x1, waiting for transfers between devices, per_device(): full_ints = lax.all_gather(cycle_ints, 'row', axis=1, tiled=True)  117 us
    dot_general x16, matrix products, product(): jnp.dot(amplitudes, columns, precision=lax.Precision.HIGHEST, preferred_e...  63.1 us
    ppermute x16, starting transfers between devices, passed_along(): lax.ppermute(x, axis, [(i, (i + by) % devices) for i in range(devices)])  30.7 us
    unnamed x3, waiting for transfers between devices  24.8 us
  transfers between devices with their start and end apart: 18, of which 18 were waited for; matrix products, arithmetic and copies ran while one was open for 0% of the time, Pallas kernels for 0%

commit v1 on v0

--- a/solution.py
+++ b/solution.py
@@ -11,7 +11,9 @@
 
 def per_device(amplitudes, cycle_ints):
     n_col = lax.axis_size("col")
-    full_ints = lax.all_gather(cycle_ints, "row", axis=1, tiled=True)
+    full_ints = jnp.concatenate(
+        lax.all_to_all(jnp.stack([cycle_ints] * lax.axis_size("row")), "row", 0, 0), axis=1
+    )
     width = full_ints.shape[1] // n_col
     here = lax.axis_index("col")
     n_rows = amplitudes.shape[0]

time: 520 us -> 496 us (0.954)
  the two profiles are of different devices: /device:TPU:16 before, /device:TPU:8 now
where the time goes in v1:
time: 496 us; the launch traced here: 494 us
  waiting for transfers between devices  358 us (72%)
  matrix products  61.7 us (12%)
  starting transfers between devices  55.3 us (11%)
  between operations  13.4 us (3%)
  local copies, waits for them, and re-layouts  5.47 us (1%)
    ppermute x16, waiting for transfers between devices, passed_along(): lax.ppermute(x, axis, [(i, (i + by) % devices) for i in range(devices)])  291 us
    dot_general x16, matrix products, product(): jnp.dot(amplitudes, columns, precision=lax.Precision.HIGHEST, preferred_e...  61.7 us
    all_to_all x1, waiting for transfers between devices, per_device(): lax.all_to_all(jnp.stack([cycle_ints] * lax.axis_size('row')), 'row', 0, 0)  43.8 us
    ppermute x16, starting transfers between devices, passed_along(): lax.ppermute(x, axis, [(i, (i + by) % devices) for i in range(devices)])  36.8 us
    unnamed x2, waiting for transfers between devices  23.6 us
    all_to_all x1, starting transfers between devices, per_device(): lax.all_to_all(jnp.stack([cycle_ints] * lax.axis_size('row')), 'row', 0, 0)  18.4 us
  transfers between devices with their start and end apart: 18, of which 18 were waited for; matrix products, arithmetic and copies ran while one was open for 0% of the time, Pallas kernels for 0%

profile of v1, /device:TPU:8, one launch (start us, length us, event | category | flops | bytes accessed | tf_op | source)
XLA Modules:
  0.0 494.4 jit_solution(16039151856179959178)
XLA Ops:
  6.5 2.2 stack.2
  8.8 0.0 copy-start
  8.8 18.4 %all-to-all-start = ((f32[8,288,144]{1,2,0:T(8,128)}), f32[8,288,144]{1,2,0:T(8,128)}, u32[]{:S(2)}, u32[]{:S(2)}) async-start(f32[8,288,144]{1,2,0:T(8,128)} %stack.2), calls=%async_computation | async-start | bytes 3538944 | tf_op jit(solution)/shard_map/all_to_all | solution.py:15
  27.2 0.0 reduce-scatter.4.cloned.1.call-start
  27.2 43.8 %all-to-all-done = f32[8,288,144]{1,2,0:T(8,128)} async-done(((f32[8,288,144]{1,2,0:T(8,128)}), f32[8,288,144]{1,2,0:T(8,128)}, u32[]{:S(2)}, u32[]{:S(2)}) %all-to-all-start) | async-done | bytes 1327136 | tf_op jit(solution)/shard_map/all_to_all | solution.py:15
  71.1 0.0 copy-done
  71.1 389.8 %while.15 = (s32[]{:T(128)}, f32[2304,72]{0,1:T(8,128)S(1)}, s32[]{:T(128)}, f32[288,1152]{0,1:T(8,128)}, f32[2304,288]{0,1:T(8,128)S(1)}, /*index=5*/s32[]{:T(1...) while((s32[]{:T(128)}, f32[2304,72]{0,1:T(8,128)S(1)}, s32[]{:T(128)}, ...), condition=%wide.region_1.2_spmd, body=%wide.region_0.1_spmd.sunk | while | flops 573474816 | bytes 6746432 | solution.py:32
  71.1 3.9 fusion.9
  75.0 1.9 collective-permute-start
  76.9 44.2 %collective-permute-done = f32[2304,72]{0,1:T(8,128)S(1)} collective-permute-done((f32[2304,72]{0,1:T(8,128)}, f32[2304,72]{0,1:T(8,128)S(1)}, u32[]{:S(2)}, u32[]{:S(2)}) %collective-permute-start) | collective-permute-done | bytes 663584 | tf_op jit(solution)/shard_map/while/body/eval_jaxpr/ppermute | solution.py:9
  121.1 3.9 fusion.9
  124.9 8.2 %collective-permute-start = (f32[2304,72]{0,1:T(8,128)}, f32[2304,72]{0,1:T(8,128)S(1)}, u32[]{:S(2)}, u32[]{:S(2)}) collective-permute-start(f32[2304,72]{0,1:T(8,128)} %fusion.9), channel_id=1, source_target_pairs={{0,4},{4,8},{8,12},{12,16},{16,20},{20,24},{24,28},{28,32},{32,36}... | collective-permute-start | bytes 1990664 | tf_op jit(solution)/shard_map/while/body/eval_jaxpr/ppermute | solution.py:9
  133.1 10.6 %collective-permute-done = f32[2304,72]{0,1:T(8,128)S(1)} collective-permute-done((f32[2304,72]{0,1:T(8,128)}, f32[2304,72]{0,1:T(8,128)S(1)}, u32[]{:S(2)}, u32[]{:S(2)}) %collective-permute-start) | collective-permute-done | bytes 663584 | tf_op jit(solution)/shard_map/while/body/eval_jaxpr/ppermute | solution.py:9
  143.7 3.9 fusion.9
  147.6 1.9 collective-permute-start
  149.5 16.9 %collective-permute-done = f32[2304,72]{0,1:T(8,128)S(1)} collective-permute-done((f32[2304,72]{0,1:T(8,128)}, f32[2304,72]{0,1:T(8,128)S(1)}, u32[]{:S(2)}, u32[]{:S(2)}) %collective-permute-start) | collective-permute-done | bytes 663584 | tf_op jit(solution)/shard_map/while/body/eval_jaxpr/ppermute | solution.py:9
  166.4 3.9 fusion.9
  170.2 1.9 collective-permute-start
  172.1 16.9 %collective-permute-done = f32[2304,72]{0,1:T(8,128)S(1)} collective-permute-done((f32[2304,72]{0,1:T(8,128)}, f32[2304,72]{0,1:T(8,128)S(1)}, u32[]{:S(2)}, u32[]{:S(2)}) %collective-permute-start) | collective-permute-done | bytes 663584 | tf_op jit(solution)/shard_map/while/body/eval_jaxpr/ppermute | solution.py:9
  189.0 3.9 fusion.9
  192.9 1.9 collective-permute-start
  194.8 16.9 %collective-permute-done = f32[2304,72]{0,1:T(8,128)S(1)} collective-permute-done((f32[2304,72]{0,1:T(8,128)}, f32[2304,72]{0,1:T(8,128)S(1)}, u32[]{:S(2)}, u32[]{:S(2)}) %collective-permute-start) | collective-permute-done | bytes 663584 | tf_op jit(solution)/shard_map/while/body/eval_jaxpr/ppermute | solution.py:9
  211.7 3.9 fusion.9
  215.5 1.9 collective-permute-start
  217.4 16.9 %collective-permute-done = f32[2304,72]{0,1:T(8,128)S(1)} collective-permute-done((f32[2304,72]{0,1:T(8,128)}, f32[2304,72]{0,1:T(8,128)S(1)}, u32[]{:S(2)}, u32[]{:S(2)}) %collective-permute-start) | collective-permute-done | bytes 663584 | tf_op jit(solution)/shard_map/while/body/eval_jaxpr/ppermute | solution.py:9
  234.3 3.9 fusion.9
  238.2 1.9 collective-permute-start
  240.1 16.9 %collective-permute-done = f32[2304,72]{0,1:T(8,128)S(1)} collective-permute-done((f32[2304,72]{0,1:T(8,128)}, f32[2304,72]{0,1:T(8,128)S(1)}, u32[]{:S(2)}, u32[]{:S(2)}) %collective-permute-start) | collective-permute-done | bytes 663584 | tf_op jit(solution)/shard_map/while/body/eval_jaxpr/ppermute | solution.py:9
  257.0 3.9 fusion.9
  260.8 1.9 collective-permute-start
  262.8 16.9 %collective-permute-done = f32[2304,72]{0,1:T(8,128)S(1)} collective-permute-done((f32[2304,72]{0,1:T(8,128)}, f32[2304,72]{0,1:T(8,128)S(1)}, u32[]{:S(2)}, u32[]{:S(2)}) %collective-permute-start) | collective-permute-done | bytes 663584 | tf_op jit(solution)/shard_map/while/body/eval_jaxpr/ppermute | solution.py:9
  279.6 3.9 fusion.9
  283.5 1.9 collective-permute-start
  285.4 16.9 %collective-permute-done = f32[2304,72]{0,1:T(8,128)S(1)} collective-permute-done((f32[2304,72]{0,1:T(8,128)}, f32[2304,72]{0,1:T(8,128)S(1)}, u32[]{:S(2)}, u32[]{:S(2)}) %collective-permute-start) | collective-permute-done | bytes 663584 | tf_op jit(solution)/shard_map/while/body/eval_jaxpr/ppermute | solution.py:9
  302.3 3.9 fusion.9
  306.1 1.9 collective-permute-start
  308.1 16.9 %collective-permute-done = f32[2304,72]{0,1:T(8,128)S(1)} collective-permute-done((f32[2304,72]{0,1:T(8,128)}, f32[2304,72]{0,1:T(8,128)S(1)}, u32[]{:S(2)}, u32[]{:S(2)}) %collective-permute-start) | collective-permute-done | bytes 663584 | tf_op jit(solution)/shard_map/while/body/eval_jaxpr/ppermute | solution.py:9
  324.9 3.9 fusion.9
  328.8 1.9 collective-permute-start
  330.7 16.9 %collective-permute-done = f32[2304,72]{0,1:T(8,128)S(1)} collective-permute-done((f32[2304,72]{0,1:T(8,128)}, f32[2304,72]{0,1:T(8,128)S(1)}, u32[]{:S(2)}, u32[]{:S(2)}) %collective-permute-start) | collective-permute-done | bytes 663584 | tf_op jit(solution)/shard_map/while/body/eval_jaxpr/ppermute | solution.py:9
  347.6 3.9 fusion.9
  351.4 1.9 collective-permute-start
  353.4 16.9 %collective-permute-done = f32[2304,72]{0,1:T(8,128)S(1)} collective-permute-done((f32[2304,72]{0,1:T(8,128)}, f32[2304,72]{0,1:T(8,128)S(1)}, u32[]{:S(2)}, u32[]{:S(2)}) %collective-permute-start) | collective-permute-done | bytes 663584 | tf_op jit(solution)/shard_map/while/body/eval_jaxpr/ppermute | solution.py:9
  370.2 3.9 fusion.9
  374.1 1.9 collective-permute-start
  376.0 16.9 %collective-permute-done = f32[2304,72]{0,1:T(8,128)S(1)} collective-permute-done((f32[2304,72]{0,1:T(8,128)}, f32[2304,72]{0,1:T(8,128)S(1)}, u32[]{:S(2)}, u32[]{:S(2)}) %collective-permute-start) | collective-permute-done | bytes 663584 | tf_op jit(solution)/shard_map/while/body/eval_jaxpr/ppermute | solution.py:9
  392.9 3.9 fusion.9
  396.8 1.9 collective-permute-start
  398.7 16.9 %collective-permute-done = f32[2304,72]{0,1:T(8,128)S(1)} collective-permute-done((f32[2304,72]{0,1:T(8,128)}, f32[2304,72]{0,1:T(8,128)S(1)}, u32[]{:S(2)}, u32[]{:S(2)}) %collective-permute-start) | collective-permute-done | bytes 663584 | tf_op jit(solution)/shard_map/while/body/eval_jaxpr/ppermute | solution.py:9
  415.5 3.9 fusion.9
  419.4 1.9 collective-permute-start
  421.3 16.9 %collective-permute-done = f32[2304,72]{0,1:T(8,128)S(1)} collective-permute-done((f32[2304,72]{0,1:T(8,128)}, f32[2304,72]{0,1:T(8,128)S(1)}, u32[]{:S(2)}, u32[]{:S(2)}) %collective-permute-start) | collective-permute-done | bytes 663584 | tf_op jit(solution)/shard_map/while/body/eval_jaxpr/ppermute | solution.py:9
  438.2 3.9 fusion.9
  442.1 1.9 collective-permute-start
  444.0 16.9 %collective-permute-done = f32[2304,72]{0,1:T(8,128)S(1)} collective-permute-done((f32[2304,72]{0,1:T(8,128)}, f32[2304,72]{0,1:T(8,128)S(1)}, u32[]{:S(2)}, u32[]{:S(2)}) %collective-permute-start) | collective-permute-done | bytes 663584 | tf_op jit(solution)/shard_map/while/body/eval_jaxpr/ppermute | solution.py:9
  460.9 1.4 copy.6
  462.2 0.0 reduce-scatter.4.cloned.1.call-update
  462.3 23.5 %reduce-scatter.4.cloned.1.call-done = f32[576,72]{1,0:T(8,128)} async-done(((f32[2304,72]{1,0:T(8,128)}), f32[576,72]{1,0:T(8,128)}) %reduce-scatter.4.cloned.1.call-update) | async-done | bytes 165904
  485.8 1.8 copy.7
  (1 shorter events, 0.0 us)
Async XLA Ops:
  8.8 62.3 %copy-start = (f32[2304,288]{0,1:T(8,128)S(1)}, f32[2304,288]{0,1:T(8,128)}, u32[]{:S(2)}) copy-start(f32[2304,288]{0,1:T(8,128)} %param.4) | copy-start | bytes 7962628
  8.8 62.2 %all-to-all-start = ((f32[8,288,144]{1,2,0:T(8,128)}), f32[8,288,144]{1,2,0:T(8,128)}, u32[]{:S(2)}, u32[]{:S(2)}) async-start(f32[8,288,144]{1,2,0:T(8,128)} %stack.2), calls=%async_computation | async-start | bytes 3538944 | tf_op jit(solution)/shard_map/all_to_all | solution.py:15
  27.2 458.6 %reduce-scatter.4.cloned.1.call-start = ((), (), s32[]{:S(2)}) async-start(), calls=%async_computation.2 | async-start | bytes 1474560
  75.0 46.1 %collective-permute-start = (f32[2304,72]{0,1:T(8,128)}, f32[2304,72]{0,1:T(8,128)S(1)}, u32[]{:S(2)}, u32[]{:S(2)}) collective-permute-start(f32[2304,72]{0,1:T(8,128)} %fusion.9), channel_id=1, source_target_pairs={{0,4},{4,8},{8,12},{12,16},{16,20},{20,24},{24,28},{28,32},{32,36}... | collective-permute-start | bytes 1990664 | tf_op jit(solution)/shard_map/while/body/eval_jaxpr/ppermute | solution.py:9
  124.9 18.8 %collective-permute-start = (f32[2304,72]{0,1:T(8,128)}, f32[2304,72]{0,1:T(8,128)S(1)}, u32[]{:S(2)}, u32[]{:S(2)}) collective-permute-start(f32[2304,72]{0,1:T(8,128)} %fusion.9), channel_id=1, source_target_pairs={{0,4},{4,8},{8,12},{12,16},{16,20},{20,24},{24,28},{28,32},{32,36}... | collective-permute-start | bytes 1990664 | tf_op jit(solution)/shard_map/while/body/eval_jaxpr/ppermute | solution.py:9
  147.6 18.8 %collective-permute-start = (f32[2304,72]{0,1:T(8,128)}, f32[2304,72]{0,1:T(8,128)S(1)}, u32[]{:S(2)}, u32[]{:S(2)}) collective-permute-start(f32[2304,72]{0,1:T(8,128)} %fusion.9), channel_id=1, source_target_pairs={{0,4},{4,8},{8,12},{12,16},{16,20},{20,24},{24,28},{28,32},{32,36}... | collective-permute-start | bytes 1990664 | tf_op jit(solution)/shard_map/while/body/eval_jaxpr/ppermute | solution.py:9
  170.2 18.8 %collective-permute-start = (f32[2304,72]{0,1:T(8,128)}, f32[2304,72]{0,1:T(8,128)S(1)}, u32[]{:S(2)}, u32[]{:S(2)}) collective-permute-start(f32[2304,72]{0,1:T(8,128)} %fusion.9), channel_id=1, source_target_pairs={{0,4},{4,8},{8,12},{12,16},{16,20},{20,24},{24,28},{28,32},{32,36}... | collective-permute-start | bytes 1990664 | tf_op jit(solution)/shard_map/while/body/eval_jaxpr/ppermute | solution.py:9
  192.9 18.8 %collective-permute-start = (f32[2304,72]{0,1:T(8,128)}, f32[2304,72]{0,1:T(8,128)S(1)}, u32[]{:S(2)}, u32[]{:S(2)}) collective-permute-start(f32[2304,72]{0,1:T(8,128)} %fusion.9), channel_id=1, source_target_pairs={{0,4},{4,8},{8,12},{12,16},{16,20},{20,24},{24,28},{28,32},{32,36}... | collective-permute-start | bytes 1990664 | tf_op jit(solution)/shard_map/while/body/eval_jaxpr/ppermute | solution.py:9
  215.5 18.8 %collective-permute-start = (f32[2304,72]{0,1:T(8,128)}, f32[2304,72]{0,1:T(8,128)S(1)}, u32[]{:S(2)}, u32[]{:S(2)}) collective-permute-start(f32[2304,72]{0,1:T(8,128)} %fusion.9), channel_id=1, source_target_pairs={{0,4},{4,8},{8,12},{12,16},{16,20},{20,24},{24,28},{28,32},{32,36}... | collective-permute-start | bytes 1990664 | tf_op jit(solution)/shard_map/while/body/eval_jaxpr/ppermute | solution.py:9
  238.2 18.8 %collective-permute-start = (f32[2304,72]{0,1:T(8,128)}, f32[2304,72]{0,1:T(8,128)S(1)}, u32[]{:S(2)}, u32[]{:S(2)}) collective-permute-start(f32[2304,72]{0,1:T(8,128)} %fusion.9), channel_id=1, source_target_pairs={{0,4},{4,8},{8,12},{12,16},{16,20},{20,24},{24,28},{28,32},{32,36}... | collective-permute-start | bytes 1990664 | tf_op jit(solution)/shard_map/while/body/eval_jaxpr/ppermute | solution.py:9
  260.8 18.8 %collective-permute-start = (f32[2304,72]{0,1:T(8,128)}, f32[2304,72]{0,1:T(8,128)S(1)}, u32[]{:S(2)}, u32[]{:S(2)}) collective-permute-start(f32[2304,72]{0,1:T(8,128)} %fusion.9), channel_id=1, source_target_pairs={{0,4},{4,8},{8,12},{12,16},{16,20},{20,24},{24,28},{28,32},{32,36}... | collective-permute-start | bytes 1990664 | tf_op jit(solution)/shard_map/while/body/eval_jaxpr/ppermute | solution.py:9
  283.5 18.8 %collective-permute-start = (f32[2304,72]{0,1:T(8,128)}, f32[2304,72]{0,1:T(8,128)S(1)}, u32[]{:S(2)}, u32[]{:S(2)}) collective-permute-start(f32[2304,72]{0,1:T(8,128)} %fusion.9), channel_id=1, source_target_pairs={{0,4},{4,8},{8,12},{12,16},{16,20},{20,24},{24,28},{28,32},{32,36}... | collective-permute-start | bytes 1990664 | tf_op jit(solution)/shard_map/while/body/eval_jaxpr/ppermute | solution.py:9
  306.1 18.8 %collective-permute-start = (f32[2304,72]{0,1:T(8,128)}, f32[2304,72]{0,1:T(8,128)S(1)}, u32[]{:S(2)}, u32[]{:S(2)}) collective-permute-start(f32[2304,72]{0,1:T(8,128)} %fusion.9), channel_id=1, source_target_pairs={{0,4},{4,8},{8,12},{12,16},{16,20},{20,24},{24,28},{28,32},{32,36}... | collective-permute-start | bytes 1990664 | tf_op jit(solution)/shard_map/while/body/eval_jaxpr/ppermute | solution.py:9
  328.8 18.8 %collective-permute-start = (f32[2304,72]{0,1:T(8,128)}, f32[2304,72]{0,1:T(8,128)S(1)}, u32[]{:S(2)}, u32[]{:S(2)}) collective-permute-start(f32[2304,72]{0,1:T(8,128)} %fusion.9), channel_id=1, source_target_pairs={{0,4},{4,8},{8,12},{12,16},{16,20},{20,24},{24,28},{28,32},{32,36}... | collective-permute-start | bytes 1990664 | tf_op jit(solution)/shard_map/while/body/eval_jaxpr/ppermute | solution.py:9
  351.4 18.8 %collective-permute-start = (f32[2304,72]{0,1:T(8,128)}, f32[2304,72]{0,1:T(8,128)S(1)}, u32[]{:S(2)}, u32[]{:S(2)}) collective-permute-start(f32[2304,72]{0,1:T(8,128)} %fusion.9), channel_id=1, source_target_pairs={{0,4},{4,8},{8,12},{12,16},{16,20},{20,24},{24,28},{28,32},{32,36}... | collective-permute-start | bytes 1990664 | tf_op jit(solution)/shard_map/while/body/eval_jaxpr/ppermute | solution.py:9
  374.1 18.8 %collective-permute-start = (f32[2304,72]{0,1:T(8,128)}, f32[2304,72]{0,1:T(8,128)S(1)}, u32[]{:S(2)}, u32[]{:S(2)}) collective-permute-start(f32[2304,72]{0,1:T(8,128)} %fusion.9), channel_id=1, source_target_pairs={{0,4},{4,8},{8,12},{12,16},{16,20},{20,24},{24,28},{28,32},{32,36}... | collective-permute-start | bytes 1990664 | tf_op jit(solution)/shard_map/while/body/eval_jaxpr/ppermute | solution.py:9
  396.8 18.8 %collective-permute-start = (f32[2304,72]{0,1:T(8,128)}, f32[2304,72]{0,1:T(8,128)S(1)}, u32[]{:S(2)}, u32[]{:S(2)}) collective-permute-start(f32[2304,72]{0,1:T(8,128)} %fusion.9), channel_id=1, source_target_pairs={{0,4},{4,8},{8,12},{12,16},{16,20},{20,24},{24,28},{28,32},{32,36}... | collective-permute-start | bytes 1990664 | tf_op jit(solution)/shard_map/while/body/eval_jaxpr/ppermute | solution.py:9
  419.4 18.8 %collective-permute-start = (f32[2304,72]{0,1:T(8,128)}, f32[2304,72]{0,1:T(8,128)S(1)}, u32[]{:S(2)}, u32[]{:S(2)}) collective-permute-start(f32[2304,72]{0,1:T(8,128)} %fusion.9), channel_id=1, source_target_pairs={{0,4},{4,8},{8,12},{12,16},{16,20},{20,24},{24,28},{28,32},{32,36}... | collective-permute-start | bytes 1990664 | tf_op jit(solution)/shard_map/while/body/eval_jaxpr/ppermute | solution.py:9
  442.1 18.8 %collective-permute-start = (f32[2304,72]{0,1:T(8,128)}, f32[2304,72]{0,1:T(8,128)S(1)}, u32[]{:S(2)}, u32[]{:S(2)}) collective-permute-start(f32[2304,72]{0,1:T(8,128)} %fusion.9), channel_id=1, source_target_pairs={{0,4},{4,8},{8,12},{12,16},{16,20},{20,24},{24,28},{28,32},{32,36}... | collective-permute-start | bytes 1990664 | tf_op jit(solution)/shard_map/while/body/eval_jaxpr/ppermute | solution.py:9
Sparse Core Ops, SparseCore 0:
  462.4 23.3 reduce-scatter.3
